TPU v7x, 32 devices: a whole 2x2x4 slice. The times are simulated.
32 devices in a mesh: gx: 8 (over z, y), gz: 2 (over x), gy: 2 (over core).
Axes of the slice: x: 2, y: 2, z: 4, core: 2. Of those that a mesh axis runs over, the one named last changes fastest.
Arguments:
- field: bfloat16 [8, 192, 96, 256], P(None, 'gx', 'gz', 'gy'), may hold values from -25 to 25
- x_factor: bfloat16 [192, 48], P('gx'), may hold values from -0.4375 to 0.4375
- y_factor: bfloat16 [256, 48], P('gy'), may hold values from -0.375 to 0.375
- species_basis_matrix: float32 [8, 4], replicated, may hold values from -2 to 2
Outputs:
- gram: float32 [96, 96], P('gz')
All inputs are finite; a program needn't handle non-finite values.
Results may differ from a plain program's by a relative error of at most 0.0003.
Values may be sent and summed in bfloat16 or wider, within the bound.
No kernel may reach another device: no remote copies, remote signals or barrier semaphores. Data moves between devices by JAX's collectives and lax.ppermute only.
A program may use at most 64 MiB of HBM per device.

v0:
```python
import jax
import jax.numpy as jnp
from jax import lax
from jax.sharding import PartitionSpec as P


def x_terms(source, x_float, planes, count):
    result = jnp.einsum("xi,nxz->niz", x_float, source, precision=lax.Precision.HIGHEST)
    return result.reshape(count, planes)


def body(field, x_factor, y_factor, species_basis_matrix):
    species_count = field.shape[0]
    breadth = field.shape[1]
    planes = field.shape[2]
    first_rank = x_factor.shape[1]
    second_rank = y_factor.shape[1]
    species_target_rank = species_basis_matrix.shape[1]
    flat = field.reshape(species_count * breadth * planes, field.shape[3])
    across_y_axis = lax.dot_general(
        y_factor, flat, (((0,), (1,)), ((), ())), preferred_element_type=jnp.float32
    )
    across_y_axis = across_y_axis.reshape(second_rank, species_count, breadth * planes)
    reduced_tensor = jnp.einsum(
        "qtb,tf->qfb", across_y_axis, species_basis_matrix, precision=lax.Precision.HIGHEST
    )
    reduced_tensor = reduced_tensor.reshape(second_rank * species_target_rank, breadth, planes)
    x_float = x_factor.astype(jnp.float32)
    share = reduced_tensor.shape[0] // (lax.axis_size("gx") * lax.axis_size("gy")) * first_rank
    core = lax.psum_scatter(
        x_terms(reduced_tensor, x_float, planes, share * lax.axis_size(("gx", "gy"))),
        ("gx", "gy"),
        scatter_dimension=0,
        tiled=True,
    )
    blocks = lax.dot_general(
        core,
        lax.all_gather(core, "gz", axis=1, tiled=True),
        (((0,), (0,)), ((), ())),
        precision=lax.Precision.HIGHEST,
        preferred_element_type=jnp.float32,
    )
    summed_tensor = lax.psum(blocks, ("gx", "gy"))
    return summed_tensor / (first_rank * second_rank * species_target_rank)


def solution(mesh):
    placed = (P(None, "gx", "gz", "gy"), P("gx", None), P("gy", None), P())
    return jax.shard_map(body, mesh=mesh, in_specs=placed, out_specs=P("gz", None), check_vma=False)
```

profile of v0, /device:TPU:0, one launch (start us, length us, event | category | flops | bytes accessed | tf_op | source)
XLA Modules:
  0.0 177.1 jit_solution(12505720334596204107)
XLA Ops:
  6.5 0.0 copy-start
  6.5 0.0 reduce-scatter.4.cloned.1.call-start
  6.5 1.7 copy-done
  8.2 0.0 copy-start.2
  8.2 1.6 fusion.1
  9.8 0.0 copy-done.2
  9.9 2.0 %convolution_bitcast_fusion = f32[48,4,1152]{2,1,0:T(4,128)S(1)} fusion(f32[48,8,1152]{2,0,1:T(8,128)S(1)} %fusion.1, f32[8,4]{0,1:T(4,128)S(1)} %copy-done.2), kind=kOutput, calls=%fused_computation | convolution fusion | flops 21233664 | bytes 2654336 | tf_op jit(solution)/shard_map/qtb,tf->qfb/dot_general | solution.py:24
  11.9 2.6 %reshape.10 = f32[192,24,48]{2,1,0:T(8,128)} reshape(f32[48,4,1152]{2,1,0:T(4,128)S(1)} %convolution_bitcast_fusion) | data formatting | bytes 1769472 | tf_op jit(solution)/shard_map/reshape | solution.py:27
  14.5 0.0 copy-start.1
  14.5 2.4 %copy.9 = f32[192,24,48]{0,1,2:T(8,128)S(1)} copy(f32[192,24,48]{2,1,0:T(8,128)} %reshape.10) | data formatting | bytes 1769472 | tf_op jit(solution)/shard_map/reshape | solution.py:27
  16.9 0.0 copy-done.1
  17.0 2.6 %convolution_bitcast_fusion.1 = f32[192,48,48]{0,1,2:T(8,128)} fusion(f32[192,24,48]{0,1,2:T(8,128)S(1)} %copy.9, bf16[24,48]{1,0:T(8,128)(2,1)S(1)} %copy-done.1), kind=kOutput, calls=%fused_computation.2 | convolution fusion | flops 127401984 | bytes 2656512 | tf_op jit(solution)/shard_map/xi,nxz->niz/dot_general | solution.py:8
  19.5 5.8 %copy.13 = f32[192,48,48]{2,1,0:T(8,128)} copy(f32[192,48,48]{0,1,2:T(8,128)} %convolution_bitcast_fusion.1) | data formatting | bytes 3538944
  25.3 0.0 reduce-scatter.4.cloned.1.call-update
  25.3 78.4 %reduce-scatter.4.cloned.1.call-done = f32[576,48]{1,0:T(8,128)} async-done(((f32[9216,48]{1,0:T(8,128)}), f32[576,48]{1,0:T(8,128)}) %reduce-scatter.4.cloned.1.call-update) | async-done | bytes 110608
  103.8 1.1 copy.12
  104.9 5.6 %all_gather.3 = f32[576,96]{0,1:T(8,128)S(1)} all-gather(f32[576,48]{0,1:T(8,128)S(1)} %copy.12), channel_id=1, replica_groups=mesh['gx'=8,'gz'=2,'gy'=2] {'gz'}, dimensions={1}, use_global_device_ids=true | all-gather | bytes 331776 | tf_op jit(solution)/shard_map/all_gather | solution.py:38
  110.4 1.6 fusion.5
  112.0 57.6 %psum.7 = f32[48,96]{1,0:T(8,128)S(1)} all-reduce(f32[48,96]{1,0:T(8,128)S(1)} %fusion.5), channel_id=1, replica_groups=mesh['gx'=8,'gz'=2,'gy'=2] {'gx','gy'}, use_global_device_ids=true, to_apply=%region_1.0 | all-reduce | flops 4608 | bytes 36864 | tf_op jit(solution)/shard_map/psum | solution.py:43
  169.7 0.6 broadcast_multiply_fusion
Async XLA Ops:
  6.5 1.7 copy-start
  6.5 97.2 %reduce-scatter.4.cloned.1.call-start = ((), (), s32[]{:S(2)}) async-start(), calls=%async_computation.1 | async-start | bytes 5013504
  8.2 1.6 copy-start.2
  14.5 2.4 %copy-start.1 = (bf16[24,48]{1,0:T(8,128)(2,1)S(1)}, bf16[24,48]{1,0:T(8,128)(2,1)}, u32[]{:S(2)}) copy-start(bf16[24,48]{1,0:T(8,128)(2,1)} %param.5) | copy-start | bytes 6916
Sparse Core Ops, SparseCore 0:
  25.5 78.2 reduce-scatter.3
where the time goes:
time: 177 us
  waiting for transfers between devices  78.5 us (44%)
  blocking collectives  63.2 us (36%)
  local copies, waits for them, and re-layouts  13.6 us (8%)
  between operations  13.4 us (8%)
  matrix products  7.83 us (4%)
    unnamed x2, waiting for transfers between devices  78.5 us
    psum x1, blocking collectives, body(): summed_tensor = lax.psum(blocks, ('gx', 'gy'))  57.6 us
    unnamed x8, local copies, waits for them, and re-layouts  8.56 us
    all_gather x1, blocking collectives, body(): lax.all_gather(core, 'gz', axis=1, tiled=True)  5.55 us
    reshape x2, local copies, waits for them, and re-layouts, body(): reduced_tensor.reshape(second_rank * species_target_rank, breadth, planes)  5.04 us
  transfers between devices with their start and end apart: 1, of which 1 were waited for; matrix products, arithmetic and copies ran while one was open for 0% of the time, Pallas kernels for 0%

commit v1 on v0

v1 whole, which is shorter than its diff:
```python
import functools

import jax
import jax.numpy as jnp
from jax import lax
from jax.experimental import pallas as pl
from jax.experimental.pallas import tpu as pltpu
from jax.sharding import PartitionSpec as P

HIGHEST = lax.Precision.HIGHEST
F32 = jnp.float32
BF16 = jnp.bfloat16
LANES = 128
FETCH = 51
PAIR = 2
HEADROOM = 14.0
VMEM = pl.BlockSpec(memory_space=pltpu.VMEM)


EVERY = ("gy", "gz", "gx")


def place_of(gx, gz, gy, groups):
    return (gy * 2 + gz) * groups + gx


def limit(mib):
    return pltpu.CompilerParams(vmem_limit_bytes=mib * 1024 * 1024)


def iota(shape, axis):
    return lax.broadcasted_iota(jnp.int32, shape, axis)


def both_parts(value):
    high = value.astype(BF16)
    return high, (value - high.astype(F32)).astype(BF16)


def columns_of(shape, share, slot):
    lane = iota(shape, 1)
    owner, place = lax.shift_right_logical(lane, slot.bit_length() - 1), lane & (slot - 1)
    return owner * share + place, place < share


def spread_y(y_rows, share, slot):
    rank = y_rows.shape[0]
    column, used = columns_of((rank, LANES), share, slot)
    row = iota((rank, LANES), 0)
    pick = jnp.where(used & ((column == row) | (column == row + rank)), 1.0, 0.0).astype(BF16)
    return lax.dot_general(y_rows, pick, (((0,), (0,)), ((), ())), preferred_element_type=F32)


def weights_of(own, share, slot, rank, basis_ref, wide):
    cores = basis_ref.shape[0] // 2
    core = lax.axis_index("gy")
    of = core if own else cores - 1 - core
    rows = [jnp.where(of == 0, basis_ref[k : k + 1, :], basis_ref[2 + k : 3 + k, :]) for k in range(2)]
    second = columns_of((1, LANES), share, slot)[0] >= rank

    def weights(species):
        blocks = []
        for s in species:
            row = jnp.where(second, rows[1][:, s : s + 1], rows[0][:, s : s + 1])
            blocks.append(jnp.concatenate(both_parts(wide * row), axis=1))
        return jnp.concatenate(blocks, axis=0)

    return weights


def fetch_kernel(field_hbm, field_ref, sems):
    copies = []
    for k in range(field_ref.shape[0]):
        copies.append(pltpu.make_async_copy(field_hbm.at[k], field_ref.at[k], sems.at[k]))
        copies[-1].start()
    for copy in copies:
        copy.wait()


def fetch(field):
    return pl.pallas_call(
        fetch_kernel,
        in_specs=[pl.BlockSpec(memory_space=pltpu.HBM)],
        out_specs=VMEM,
        out_shape=jax.ShapeDtypeStruct(field.shape, field.dtype),
        scratch_shapes=[pltpu.SemaphoreType.DMA((field.shape[0],))],
        compiler_params=limit(FETCH),
    )(field)


def multiply(weights, field_ref, out_ref, sum_ref):
    species, breadth, planes, depth = field_ref.shape
    for k in range(0, species, PAIR):
        lhs = [field_ref[k + s].reshape(breadth * planes, depth) for s in range(PAIR)]
        held = weights(range(k, k + PAIR))
        both = jnp.dot(jnp.concatenate(lhs, axis=1), held, preferred_element_type=F32)
        if k > 0:
            both = both + sum_ref[...]
        if k + PAIR < species:
            sum_ref[...] = both
        else:
            out_ref[...] = both[:, :LANES] + both[:, LANES:]


def far_kernel(share, slot, basis_ref, y_ref, field_ref, out_ref, wide_ref, sum_ref):
    wide = spread_y(y_ref[...], share, slot)
    wide_ref[...] = wide
    multiply(weights_of(False, share, slot, y_ref.shape[0], basis_ref, wide), field_ref, out_ref, sum_ref)


def own_kernel(share, slot, rank, basis_ref, wide_ref, field_ref, out_ref, sum_ref):
    weights = weights_of(True, share, slot, rank, basis_ref, wide_ref[...])
    multiply(weights, field_ref, out_ref, sum_ref)


def project(kernel, basis_rows, y_values, field, more_out=()):
    _, breadth, planes, _ = field.shape
    out = [jax.ShapeDtypeStruct((breadth * planes, LANES), F32), *more_out]
    return pl.pallas_call(
        kernel,
        in_specs=[VMEM] * 3,
        out_specs=[VMEM] * len(out),
        out_shape=out,
        scratch_shapes=[pltpu.VMEM((breadth * planes, 2 * LANES), F32)],
        compiler_params=limit(32),
    )(basis_rows, y_values, field)


def exponent(value):
    largest = jnp.max(jnp.abs(value), axis=(0, 1), keepdims=True)
    return jnp.ceil(jnp.log2(jnp.maximum(largest, 2.0**-100)))


def trade(slot, owners, tiles):
    lane = iota(tiles[0].shape, 1)
    turned = [tile if z == 0 else pltpu.roll(tile, slot * z, 1) for z, tile in enumerate(tiles)]
    bit = 1
    while bit < owners:
        upper = (lane & (bit * slot)) != 0
        turned = [jnp.where(upper, turned[(n + bit) % owners], turned[n]) for n in range(owners)]
        bit *= 2
    picked = [turned[-k % owners] for k in range(owners)]
    return [tile if k == 0 else pltpu.roll(tile, LANES - slot * k, 1) for k, tile in enumerate(picked)]


def largest_of(ref):
    return jnp.max(jnp.abs(ref[...]).reshape(-1, 8, LANES), axis=0)


def trade_kernel(slot, mine_ref, x_ref, out_ref, largest_ref, ride_ref, power_ref):
    owners, breadth, width = out_ref.shape
    planes = width // slot
    rank = x_ref.shape[1]
    largest_ref[...] = largest_of(mine_ref)
    for g in range(planes // owners):
        rows = [pl.ds(g * owners + k, breadth, stride=planes) for k in range(owners)]
        for k, tile in enumerate(trade(slot, owners, [mine_ref[r, :] for r in rows])):
            out_ref[k, :, pl.ds(g * LANES, LANES)] = tile
    x_rows = x_ref[...].astype(F32)
    power = exponent(x_rows)
    x_rows = (x_rows * jnp.exp2(-power)).astype(BF16)
    place = jnp.where(iota((rank, width), 1) == iota((rank, width), 0) * slot + slot - 1, 1.0, 0.0)
    rides = jnp.dot(x_rows, place.astype(BF16), preferred_element_type=F32)
    turn = lax.axis_index("gz") * 2 + lax.axis_index("gy")
    part = rides[:8]
    for n in range(1, breadth // 8):
        part = jnp.where(turn == n, rides[8 * n : 8 * n + 8], part)
    ride_ref[...] = part
    power_ref[...] = jnp.broadcast_to(power, power_ref.shape)


def spread_own(mine, x_factor, slot):
    owners = LANES // slot
    breadth = x_factor.shape[0]
    planes = mine.shape[0] // breadth
    shapes = [(owners, breadth, planes * slot), (8, LANES), (8, planes * slot), (8, LANES)]
    return pl.pallas_call(
        functools.partial(trade_kernel, slot),
        in_specs=[VMEM] * 2,
        out_specs=[VMEM] * 4,
        out_shape=[jax.ShapeDtypeStruct(shape, F32) for shape in shapes],
        compiler_params=limit(32),
    )(mine, x_factor)


def pack(core, tiles, slot, share, x_tiles, powers):
    half, lane = share // 2, iota(tiles[0].shape, 1)
    place = lane & (slot - 1)
    packed = []
    for left, right in zip(tiles[0:-1:2], tiles[1:-1:2]):
        if core == 0:
            right = pltpu.roll(right, half, 1)
        else:
            left = pltpu.roll(left, LANES - half, 1)
        packed.append(jnp.where(place < half, left, right))
    for j in range(half):
        moved = pltpu.roll(tiles[-1], share - core * half - j, 1)
        packed[j] = jnp.where(place == share, moved, packed[j])
    for g, tile in enumerate(x_tiles):
        packed[g] = jnp.where(place == slot - 1, tile, packed[g])
    for n, power in enumerate(powers):
        packed[-1] = jnp.where(lane == n * slot + share, power, packed[-1])
    return packed


def unpack(packed, slot, share):
    half = share // 2
    place = iota(packed[0][0].shape, 1) & (slot - 1)
    tiles = []
    for first, second in zip(*packed):
        tiles.append(jnp.where(place < half, first, pltpu.roll(second, half, 1)))
        tiles.append(jnp.where(place < half, pltpu.roll(first, LANES - half, 1), second))
    last = jnp.zeros_like(tiles[0])
    for column in range(share):
        moved = pltpu.roll(packed[column // half][column % half], LANES - share + column, 1)
        last = jnp.where(place == column, moved, last)
    return tiles + [last]


def spread_kernel(slot, share, mine_ref, largest_ref, ride_ref, power_ref, other_ref, out_ref, sum_ref):
    owners, breadth, width = mine_ref.shape
    planes = width // slot
    power = exponent(largest_ref[...] + largest_of(other_ref))
    factor = jnp.exp2(HEADROOM - power)
    x_tiles = [ride_ref[:, pl.ds(c, LANES)] for c in range(0, width, LANES)]
    for g in range(planes // owners):
        rows = [pl.ds(g * owners + k, breadth, stride=planes) for k in range(owners)]
        lanes = pl.ds(g * LANES, LANES)
        for k, tile in enumerate(trade(slot, owners, [other_ref[r, :] for r in rows])):
            sum_ref[k, :, lanes] = (mine_ref[k, :, lanes] + tile) * factor
    for k in range(owners):
        tiles = [
            sum_ref[k, pl.ds(r, 8), pl.ds(c, LANES)]
            for r in range(0, breadth, 8)
            for c in range(0, width, LANES)
        ]
        for core in range(2):
            for t, tile in enumerate(pack(core, tiles, slot, share, x_tiles, (power, power_ref[...]))):
                out_ref[place_of(k // 2, k % 2, core, owners // 2), pl.ds(8 * t, 8), :] = tile


def spread(mine, other, slot, share):
    owners, breadth, width = mine[0].shape
    return pl.pallas_call(
        functools.partial(spread_kernel, slot, share),
        in_specs=[VMEM] * 5,
        out_specs=VMEM,
        out_shape=jax.ShapeDtypeStruct((2 * owners, breadth * width // LANES // 16 * 8, LANES), F32),
        scratch_shapes=[pltpu.VMEM(mine[0].shape, F32)],
        compiler_params=limit(32),
    )(*mine, other)


def gram_kernel(groups, share, slot, scale, parts_ref, out_ref, core_ref, rows_ref, wide_ref, factor_ref):
    senders, height, _ = parts_ref.shape
    blocks = senders // groups // 2
    width = core_ref.shape[0] // blocks
    planes = width // slot
    rank = core_ref.shape[1]
    across = width // LANES
    take = jnp.where(iota((width, rank), 0) == iota((width, rank), 1) * slot + slot - 1, 1.0, 0.0)
    take = take.astype(BF16)
    is_x = (iota((8, LANES), 1) & (slot - 1)) == slot - 1
    for d in range(senders):
        factor_ref[pl.ds(d, 1), :] = parts_ref[d, pl.ds(height - 8, 1), :]
    rows = factor_ref[...]
    lane = iota(rows.shape, 1)
    powers = jnp.where(lane == slot + share, jnp.exp2(rows), 0.0)
    powers = jnp.where(lane == share, jnp.exp2(rows - HEADROOM), powers)
    lane, row = iota((LANES, LANES), 1) & (slot - 1), iota((LANES, LANES), 0)
    given = jnp.where(lane == slot - 1, slot + share, share)
    spread_to = jnp.where(row == given, 1.0, 0.0).astype(BF16)
    factor_ref[...] = jnp.dot(powers.astype(BF16), spread_to, preferred_element_type=F32)
    chunks = [[] for _ in range(blocks)]
    for g in range(groups):
        packed = []
        for s in range(2 * blocks):
            at = place_of(g, s // 2, s % 2, groups)
            factor = factor_ref[pl.ds(at, 1), :]
            packed.append([parts_ref[at, pl.ds(r, 8), :] * factor for r in range(0, height, 8)])
        for b in range(blocks):
            tiles = unpack(packed[2 * b : 2 * b + 2], slot, share)
            if b == 0:
                for t in range(len(tiles)):
                    tiles[t] = jnp.where(is_x, packed[t // across][t % across], tiles[t])
            for t in range(0, len(tiles), across):
                chunks[b].append(jnp.concatenate(tiles[t : t + across], axis=1))
    x_all = None
    for b in range(blocks):
        high, low = both_parts(jnp.concatenate(chunks[b], axis=0))
        if x_all is None:
            x_all = jnp.dot(high, take, preferred_element_type=F32).astype(BF16)
        dims = (((0,), (0,)), ((), ()))
        core = lax.dot_general(high, x_all, dims, preferred_element_type=F32)
        core = core + lax.dot_general(low, x_all, dims, preferred_element_type=F32)
        core_ref[pl.ds(b * width, width), :] = core
    rows_ref[...] = jnp.zeros_like(rows_ref)
    for c in range(share):
        for b in range(blocks):
            rows = core_ref[pl.ds(b * width + c, planes, stride=slot), :]
            rows_ref[pl.ds(b * planes, planes), pl.ds(c * LANES, rank)] = rows
    high, low = both_parts(rows_ref[...])
    dims = (((1,), (1,)), ((), ()))
    cross = lax.dot_general(high, low, dims, preferred_element_type=F32)
    gram = lax.dot_general(high, high, dims, preferred_element_type=F32)
    gram = (gram + cross + cross.T) * scale
    power = exponent(gram)
    wide_ref[...] = jnp.broadcast_to(power, wide_ref.shape)
    wide_ref[:, : blocks * planes] = gram * jnp.exp2(HEADROOM - power)
    copies, height, _ = out_ref.shape
    wide = [wide_ref[pl.ds(start, height), :] for start in range(0, blocks * planes, height)]
    for d in range(copies):
        out_ref[d] = wide[d // groups % 2 * 2 + d // groups // 2]


def gram_rows(parts, groups, planes, rank, share, slot, scale):
    blocks = parts.shape[0] // groups // 2
    width = planes * slot
    return pl.pallas_call(
        functools.partial(gram_kernel, groups, share, slot, scale),
        in_specs=[VMEM],
        out_specs=VMEM,
        out_shape=jax.ShapeDtypeStruct((parts.shape[0], planes // 2, LANES), F32),
        scratch_shapes=[
            pltpu.VMEM((blocks * width, rank), F32),
            pltpu.VMEM((blocks * planes, share * LANES), F32),
            pltpu.VMEM((blocks * planes, LANES), F32),
            pltpu.VMEM((parts.shape[0], LANES), F32),
        ],
        compiler_params=limit(32),
    )(parts)


def sum_kernel(parts_ref, out_ref):
    width = out_ref.shape[1]
    total = 0.0
    for d in range(parts_ref.shape[0]):
        power = parts_ref[d, :, width : width + 1]
        total = total + parts_ref[d, :, :width] * jnp.exp2(power - HEADROOM)
    out_ref[...] = total


def sum_parts(parts, width):
    return pl.pallas_call(
        sum_kernel,
        in_specs=[VMEM],
        out_specs=VMEM,
        out_shape=jax.ShapeDtypeStruct((parts.shape[1], width), F32),
        compiler_params=limit(32),
    )(parts)


def join_kernel(own_ref, other_ref, out_ref):
    first = lax.axis_index("gy") == 0
    half = own_ref.shape[0]
    out_ref[:half] = jnp.where(first, own_ref[...], other_ref[...])
    out_ref[half:] = jnp.where(first, other_ref[...], own_ref[...])


def join(own, other):
    return pl.pallas_call(
        join_kernel,
        in_specs=[VMEM] * 2,
        out_specs=VMEM,
        out_shape=jax.ShapeDtypeStruct((2 * own.shape[0], own.shape[1]), F32),
        compiler_params=limit(32),
    )(own, other)


def swap_with_all(value, axes):
    return lax.all_to_all(value, axes, split_axis=0, concat_axis=0, tiled=True)


def swap_cores(value):
    return lax.ppermute(value, "gy", [(0, 1), (1, 0)])


def fast_body(field, x_factor, y_factor, species_basis_matrix):
    planes = field.shape[2]
    first_rank, second_rank = x_factor.shape[1], y_factor.shape[1]
    target_rank = species_basis_matrix.shape[1]
    gx, gz, gy = (lax.axis_size(name) for name in ("gx", "gz", "gy"))
    owners = gx * gz
    slot = LANES // owners
    share = target_rank * second_rank // (owners * gy)
    y_rows, basis_rows = y_factor.T, species_basis_matrix.T
    held = fetch(field)
    far, wide = project(
        functools.partial(far_kernel, share, slot),
        basis_rows,
        y_rows,
        held,
        [jax.ShapeDtypeStruct((y_rows.shape[1], LANES), F32)],
    )
    other = swap_cores(far)
    (mine,) = project(functools.partial(own_kernel, share, slot, second_rank), basis_rows, wide, held)
    chunks = spread(spread_own(mine, x_factor, slot), other, slot, share)
    parts = swap_with_all(chunks.astype(jnp.float16), EVERY).astype(F32)
    scale = 1.0 / (first_rank * second_rank * target_rank)
    rows = gram_rows(parts, gx, planes, first_rank, share, slot, scale)
    rows = swap_with_all(rows.astype(jnp.float16), EVERY).astype(F32)
    rows = sum_parts(rows, gz * planes)
    return join(rows, swap_cores(rows))


def any_body(field, x_factor, y_factor, species_basis_matrix):
    species_count, breadth, planes, depth = field.shape
    first_rank = x_factor.shape[1]
    second_rank = y_factor.shape[1]
    target_rank = species_basis_matrix.shape[1]
    gx, gz, gy = (lax.axis_size(name) for name in ("gx", "gz", "gy"))
    z_at, y_at = lax.axis_index("gz"), lax.axis_index("gy")
    flat = field.reshape(species_count * breadth * planes, depth)
    across_y = lax.dot_general(
        y_factor, flat, (((0,), (1,)), ((), ())), preferred_element_type=F32
    ).reshape(second_rank, species_count, breadth * planes)
    reduced = jnp.einsum("qtb,tf->fqb", across_y, species_basis_matrix, precision=HIGHEST)
    reduced = reduced.reshape(target_rank * second_rank, breadth, planes)
    half = reduced.shape[0] // gy
    mine = lax.dynamic_slice_in_dim(reduced, y_at * half, half, 0)
    for step in range(1, gy):
        other = lax.dynamic_slice_in_dim(reduced, lax.rem(y_at + step, gy) * half, half, 0)
        mine = mine + lax.ppermute(other, "gy", [(i, (i + step) % gy) for i in range(gy)])
    group = gx * gz
    share = -(-half // group)
    mine = jnp.pad(mine, ((0, share * group - half), (0, 0), (0, 0)))
    whole_x = lax.all_gather(x_factor, "gx", axis=0, tiled=True).astype(F32)
    parts = swap_with_all(mine.reshape(group, share, breadth, planes), ("gx", "gz"))
    parts = parts.reshape(gx, gz, share, breadth, planes)
    core = jnp.einsum("asi,abpsz->bzpi", whole_x.reshape(gx, breadth, first_rank), parts, precision=HIGHEST)
    core = core.reshape(gz * planes, share * first_rank)
    gram = lax.dot_general(core, core, (((1,), (1,)), ((), ())), precision=HIGHEST)
    gram = lax.psum_scatter(gram, "gz", scatter_dimension=0, tiled=True)
    return lax.psum(gram, ("gx", "gy")) / (first_rank * second_rank * target_rank)


def body(field, x_factor, y_factor, species_basis_matrix):
    _, breadth, planes, depth = field.shape
    gx, gz, gy = (lax.axis_size(name) for name in ("gx", "gz", "gy"))
    owners = gx * gz
    columns = species_basis_matrix.shape[1] * y_factor.shape[1]
    fits = (
        gx > 1
        and gy == 2
        and gz == 2
        and owners == 16
        and columns == 6 * owners * gy
        and species_basis_matrix.shape[1] == 2 * gy
        and breadth == 24
        and planes == 3 * owners
        and planes == x_factor.shape[1]
        and field.shape[0] % PAIR == 0
        and depth == LANES
    )
    return (fast_body if fits else any_body)(field, x_factor, y_factor, species_basis_matrix)


def solution(mesh):
    placed = (P(None, "gx", "gz", "gy"), P("gx", None), P("gy", None), P())
    return jax.shard_map(body, mesh=mesh, in_specs=placed, out_specs=P("gz", None), check_vma=False)
```

time: 177 us -> 38.6 us (0.22)
  waiting for transfers between devices: 78.5 us -> 1.01 us
  blocking collectives: 63.2 us -> 28.4 us
  local copies, waits for them, and re-layouts: 13.6 us -> 0.01 us
  between operations: 13.4 us -> 0.1 us
  matrix products: 7.83 us -> 0 us
  Pallas kernels: 0 us -> 7.1 us
    unnamed x2 -> x0, waiting for transfers between devices: 78.5 us -> none
    psum x1 -> x0, blocking collectives: 57.6 us -> none  [body(): summed_tensor = lax.psum(blocks, ('gx', 'gy'))]
    all_to_all x0 -> x2, blocking collectives: none -> 28.4 us  [swap_with_all(): return lax.all_to_all(value, axes, split_axis=0, concat_axis=0, tiled=True)]
    unnamed x8 -> x6, local copies, waits for them, and re-layouts: 8.56 us -> 0.01 us
    dot_general x4 -> x0, matrix products: 7.83 us -> none  [the longest x1 2.57 us: x_terms(): jnp.einsum('xi,nxz->niz', x_float, source, precision=lax.Precision.HIGHEST)]
    pallas_call x0 -> x8, Pallas kernels: none -> 7.1 us  [the longest x2 1.82 us: project(): pl.pallas_call(kernel, in_specs=[VMEM] * 3, out_specs=[VMEM] * len(out),...]
    all_gather x1 -> x0, blocking collectives: 5.55 us -> none  [body(): lax.all_gather(core, 'gz', axis=1, tiled=True)]
    reshape x2 -> x0, local copies, waits for them, and re-layouts: 5.04 us -> none  [body(): reduced_tensor.reshape(second_rank * species_target_rank, breadth, planes)]
  transfers between devices with their start and end apart: 1 -> 2, of which waited for: 1 -> 2; matrix products, arithmetic and copies ran while one was open for 0% -> 0% of each run, Pallas kernels for 0% -> 4%
where the time goes in v1:
time: 38.6 us; the launch traced here: 38.4 us
  blocking collectives  28.4 us (74%)
  Pallas kernels  7.1 us (18%)
  starting transfers between devices  1.67 us (4%)
  waiting for transfers between devices  1.01 us (3%)
    all_to_all x2, blocking collectives, swap_with_all(): return lax.all_to_all(value, axes, split_axis=0, concat_axis=0, tiled=True)  28.4 us
    pallas_call x2, Pallas kernels, project(): pl.pallas_call(kernel, in_specs=[VMEM] * 3, out_specs=[VMEM] * len(out),...  1.82 us
    pallas_call x1, Pallas kernels, fetch(): pl.pallas_call(fetch_kernel, in_specs=[pl.BlockSpec(memory_space=pltpu.HB...  1.67 us
    ppermute x2, starting transfers between devices, swap_cores(): return lax.ppermute(value, 'gy', [(0, 1), (1, 0)])  1.67 us
    pallas_call x1, Pallas kernels, gram_rows(): pl.pallas_call(functools.partial(gram_kernel, groups, share, slot, scale)...  1.39 us
    ppermute x2, waiting for transfers between devices, swap_cores(): return lax.ppermute(value, 'gy', [(0, 1), (1, 0)])  1.01 us
    pallas_call x1, Pallas kernels, spread(): pl.pallas_call(functools.partial(spread_kernel, slot, share), in_specs=[V...  0.85 us
  transfers between devices with their start and end apart: 2, of which 2 were waited for; matrix products, arithmetic and copies ran while one was open for 0% of the time, Pallas kernels for 4%

profile of v1, /device:TPU:0, one launch (start us, length us, event | category | flops | bytes accessed | tf_op | source)
XLA Modules:
  0.0 38.4 jit_solution(13939303856728358643)
XLA Ops:
  0.0 0.0 copy-start.1
  0.0 0.0 copy-start
  0.0 1.7 %shard_map.46.field_ref = bf16[8,24,48,128]{3,2,1,0:T(8,128)(2,1)S(1)} custom-call(bf16[8,24,48,128]{3,2,1,0:T(8,128)(2,1)} %field_hbm.1), custom_call_target="tpu_custom_call" | custom-call | tf_op jit(solution)/shard_map/pallas_call | solution.py:81
  1.7 0.0 copy-done.1
  1.7 0.0 copy-done
  1.7 0.0 copy-start.2
  1.7 1.0 %shard_map.47 = (f32[1152,128]{1,0:T(8,128)S(1)}, f32[128,128]{1,0:T(8,128)S(1)}) custom-call(f32[4,8]{1,0:T(4,128)S(1)} %bitcast.3, bf16[48,128]{1,0:T(8,128)(2,1)S(1)} %bitcast.2, bf16[8,24,48,128]{3,2,1,0:T(8,128)(2,1)S(1)} %shard_map.46.field_ref), custom_call_target="tpu_custom_call" | custom-call | tf_op jit(solution)/shard_map/pallas_call | solution.py:119
  2.7 0.5 %collective-permute-start = (f32[1152,128]{1,0:T(8,128)S(1)}, f32[1152,128]{1,0:T(8,128)S(1)}, u32[]{:S(2)}, u32[]{:S(2)}) collective-permute-start(f32[1152,128]{1,0:T(8,128)S(1)} %get-tuple-element.16), channel_id=1, source_target_pairs={{0,1},{1,0},{2,3},{3,2},{4,5},{5,4},{6,7},{7,6},{8,9},{9,8},{10,11... | collective-permute-start | bytes 1769480 | tf_op jit(solution)/shard_map/ppermute | solution.py:375
  3.2 0.9 %shard_map.48.mine_ref = f32[1152,128]{1,0:T(8,128)S(1)} custom-call(f32[4,8]{1,0:T(4,128)S(1)} %bitcast.4, f32[128,128]{1,0:T(8,128)S(1)} %get-tuple-element.11.wide_ref, bf16[8,24,48,128]{3,2,1,0:T(8,128)(2,1)S(1)} %shard_map.46.field_ref), custom_call_target="tpu_custom_call" | custom-call | tf_op jit(solution)/shard_map/pallas_call | solution.py:119
  4.1 0.0 copy-done.2
  4.1 0.6 %shard_map.49 = (f32[16,24,384]{2,1,0:T(8,128)S(1)}, f32[8,128]{1,0:T(8,128)S(1)}, f32[8,384]{1,0:T(8,128)S(1)}, f32[8,128]{1,0:T(8,128)S(1)}) custom-call(f32[1152,128]{1,0:T(8,128)S(1)} %shard_map.48.mine_ref, bf16[24,48]{1,0:T(8,128)(2,1)S(1)} %copy-done.2), custom_call_target="tpu_custom_call" | custom-call | tf_op jit(solution)/shard_map/pallas_call | solution.py:177
  4.7 0.2 collective-permute-done.other_ref
  4.8 0.8 %shard_map.50 = f32[32,32,128]{2,1,0:T(8,128)S(1)} custom-call(f32[16,24,384]{2,1,0:T(8,128)S(1)} %get-tuple-element.12.mine_ref, f32[8,128]{1,0:T(8,128)S(1)} %get-tuple-element.13.largest_ref, f32[8,384]{1,0:T(8,128)S(1)} %get-tuple-element.14.ride_ref, f32[8,128]{1,0:T(8,128)S(1)} %get-tuple-element.15.power_ref, ...), custom_call_target="tpu_custom_call" | custom-call | tf_op jit(solution)/shard_map/pallas_call | solution.py:244
  5.7 17.7 %all_to_all.10 = f16[32,32,128]{2,1,0:T(8,128)(2,1)S(1)} all-to-all(f16[32,32,128]{2,1,0:T(8,128)(2,1)S(1)} %convert_element_type.12), channel_id=1, replica_groups=mesh['gx'=8,'gz'=2,'gy'=2] {'gy','gz','gx'}, dimensions={0} | all-to-all | bytes 524288 | tf_op jit(solution)/shard_map/all_to_all | solution.py:371
  23.4 0.1 convert_element_type.13.parts_ref
  23.5 1.4 %shard_map.51 = f32[32,24,128]{2,1,0:T(8,128)S(1)} custom-call(f32[32,32,128]{2,1,0:T(8,128)S(1)} %convert_element_type.13.parts_ref), custom_call_target="tpu_custom_call" | custom-call | tf_op jit(solution)/shard_map/pallas_call | solution.py:319
  24.9 10.7 %all_to_all.11 = f16[32,24,128]{2,1,0:T(8,128)(2,1)S(1)} all-to-all(f16[32,24,128]{2,1,0:T(8,128)(2,1)S(1)} %convert_element_type.14), channel_id=1, replica_groups=mesh['gx'=8,'gz'=2,'gy'=2] {'gy','gz','gx'}, dimensions={0} | all-to-all | bytes 393216 | tf_op jit(solution)/shard_map/all_to_all | solution.py:371
  35.7 0.2 shard_map.52.own_ref
  35.8 1.2 %collective-permute-start.1 = (f32[24,96]{1,0:T(8,128)S(1)}, f32[24,96]{1,0:T(8,128)S(1)}, u32[]{:S(2)}, u32[]{:S(2)}) collective-permute-start(f32[24,96]{1,0:T(8,128)S(1)} %shard_map.52.own_ref), channel_id=1, source_target_pairs={{0,1},{1,0},{2,3},{3,2},{4,5},{5,4},{6,7},{7,6},{8,9},{9,8},{10,11... | collective-permute-start | bytes 27656 | tf_op jit(solution)/shard_map/ppermute | solution.py:375
  37.0 0.8 %collective-permute-done.1.other_ref = f32[24,96]{1,0:T(8,128)S(1)} collective-permute-done((f32[24,96]{1,0:T(8,128)S(1)}, f32[24,96]{1,0:T(8,128)S(1)}, u32[]{:S(2)}, u32[]{:S(2)}) %collective-permute-start.1) | collective-permute-done | bytes 9248 | tf_op jit(solution)/shard_map/ppermute | solution.py:375
  37.8 0.6 %shard_map.53 = f32[48,96]{1,0:T(8,128)} custom-call(f32[24,96]{1,0:T(8,128)S(1)} %shard_map.52.own_ref, f32[24,96]{1,0:T(8,128)S(1)} %collective-permute-done.1.other_ref), custom_call_target="tpu_custom_call" | custom-call | tf_op jit(solution)/shard_map/pallas_call | solution.py:361
  (3 shorter events, 0.1 us)
Async XLA Ops:
  0.0 1.7 %copy-start.1 = (f32[8,4]{0,1:T(4,128)S(1)}, f32[8,4]{0,1:T(4,128)}, u32[]{:S(2)}) copy-start(f32[8,4]{0,1:T(4,128)} %param.7) | copy-start | bytes 388
  0.0 1.7 %copy-start = (bf16[128,48]{0,1:T(8,128)(2,1)S(1)}, bf16[128,48]{0,1:T(8,128)(2,1)}, u32[]{:S(2)}) copy-start(bf16[128,48]{0,1:T(8,128)(2,1)} %param.6) | copy-start | bytes 36868
  1.7 2.4 %copy-start.2 = (bf16[24,48]{1,0:T(8,128)(2,1)S(1)}, bf16[24,48]{1,0:T(8,128)(2,1)}, u32[]{:S(2)}) copy-start(bf16[24,48]{1,0:T(8,128)(2,1)} %x_ref.1) | copy-start | bytes 6916
  2.7 2.2 %collective-permute-start = (f32[1152,128]{1,0:T(8,128)S(1)}, f32[1152,128]{1,0:T(8,128)S(1)}, u32[]{:S(2)}, u32[]{:S(2)}) collective-permute-start(f32[1152,128]{1,0:T(8,128)S(1)} %get-tuple-element.16), channel_id=1, source_target_pairs={{0,1},{1,0},{2,3},{3,2},{4,5},{5,4},{6,7},{7,6},{8,9},{9,8},{10,11... | collective-permute-start | bytes 1769480 | tf_op jit(solution)/shard_map/ppermute | solution.py:375
  35.8 2.0 %collective-permute-start.1 = (f32[24,96]{1,0:T(8,128)S(1)}, f32[24,96]{1,0:T(8,128)S(1)}, u32[]{:S(2)}, u32[]{:S(2)}) collective-permute-start(f32[24,96]{1,0:T(8,128)S(1)} %shard_map.52.own_ref), channel_id=1, source_target_pairs={{0,1},{1,0},{2,3},{3,2},{4,5},{5,4},{6,7},{7,6},{8,9},{9,8},{10,11... | collective-permute-start | bytes 27656 | tf_op jit(solution)/shard_map/ppermute | solution.py:375
